TPU v7x, 32 devices: a whole 2x2x4 slice. The times are simulated.
32 devices in a mesh: sta: 32 (over z, y, x, core).
Axes of the slice: x: 2, y: 2, z: 4, core: 2. Of those that a mesh axis runs over, the one named last changes fastest.
Arguments:
- records: bfloat16 [2560, 2048], P('sta'), may hold values from -6 to 6
- green: bfloat16 [2560, 2048], P('sta'), may hold values from -4 to 4
- pair_mask: int32 [2560, 720], P('sta'), may hold values 0 or 1
- tile_lists: int32 [2560, 16], P('sta'), may hold values from 0 to 127
- tile_weights: float32 [2560, 16], P('sta'), may hold values from -0.3125 to 0.3125
- tile_green: bfloat16 [65536, 1024], P('sta'), may hold values from -0.125 to 0.125
Outputs:
- adjoint: bfloat16 [2560, 2048], P('sta')
- kernel: float32 [128, 1024], P('sta')
All inputs are finite; a program needn't handle non-finite values. No bound on the sum of `pair_mask` on one device may be relied on, other than what follows from the above.
Results may differ from a plain program's by a relative error of at most 0.0034.
Values may be sent and summed in bfloat16 or wider, within the bound.
A program may use at most 64 MiB of HBM per device.

v0:
```python
import jax
import jax.numpy as jnp
from jax import lax
from jax.sharding import PartitionSpec as P

C = 80
F = 1024
TT = 4
HALF = 4
WIN = 9


def passed_along(value, axis, steps):
    count = lax.axis_size(axis)
    pairs = [(source, (source + steps) % count) for source in range(count)]
    return lax.ppermute(value, axis, pairs)


def add_block(totals, mask_bf, moving, offset):
    columns = mask_bf[:, offset * C : (offset + 1) * C]
    return (
        totals[0] + jnp.dot(columns, moving[0], preferred_element_type=jnp.float32),
        totals[1] + jnp.dot(columns, moving[1], preferred_element_type=jnp.float32),
    )


def local(records, green, pair_mask, tile_lists, tile_weights, tile_green):
    rec = records.astype(jnp.float32)
    grn = green.astype(jnp.float32)
    rec_real, rec_imag = (rec[:, :F], rec[:, F:])
    green_real, green_imag = (grn[:, :F], grn[:, F:])
    cross = jnp.concatenate(
        [
            rec_real * green_real + rec_imag * green_imag,
            rec_real * green_imag - rec_imag * green_real,
        ],
        axis=1,
    ).astype(jnp.bfloat16)
    power = (green_real * green_real + green_imag * green_imag).astype(jnp.bfloat16)
    mask_bf = pair_mask.astype(jnp.bfloat16)
    totals = (jnp.zeros((C, 2 * F), jnp.float32), jnp.zeros((C, F), jnp.float32))
    totals = add_block(totals, mask_bf, (cross, power), HALF)
    moving = passed_along((cross, power), "sta", -HALF)
    totals = add_block(totals, mask_bf, moving, 2 * HALF)
    for stepper in range(2 * HALF):
        moving = passed_along((moving[0], moving[1]), "sta", 1)
        offset = 2 * HALF - 1 - stepper
        if offset != HALF:
            totals = add_block(totals, mask_bf, moving, offset)
    factor = 1.0 / jnp.sqrt(jnp.float32(WIN * C))
    qsum = totals[0] * factor
    psum = totals[1] * factor
    q_real, q_imag = (qsum[:, :F], qsum[:, F:])
    adj_real = rec_real * q_real - rec_imag * q_imag - green_real * psum
    adj_imag = rec_real * q_imag + rec_imag * q_real - green_imag * psum
    adjoint = jnp.concatenate([adj_real, adj_imag], axis=1).astype(jnp.bfloat16)
    tiles_total = TT * lax.axis_size("sta")
    tile_ids = jnp.arange(tiles_total, dtype=jnp.int32)
    onehot = (tile_lists[None, :, :] == tile_ids[:, None, None]).astype(jnp.float32)
    tile_map = jnp.sum(onehot * tile_weights[None, :, :], axis=2)
    spread = jnp.dot(tile_map, adjoint.astype(jnp.float32), precision=lax.Precision.HIGHEST)
    green_wide = tile_green.astype(jnp.float32)
    kernel = lax.psum_scatter(
        jnp.dot(spread, green_wide, precision=lax.Precision.HIGHEST),
        "sta",
        scatter_dimension=0,
        tiled=True,
    )
    return (adjoint, kernel)


def solution(mesh):
    placed = (
        P("sta", None),
        P("sta", None),
        P("sta", None),
        P("sta", None),
        P("sta", None),
        P("sta", None),
    )
    return jax.shard_map(
        local,
        mesh=mesh,
        in_specs=placed,
        out_specs=(P("sta", None), P("sta", None)),
        check_vma=False,
    )
```

profile of v0, /device:TPU:0, one launch (start us, length us, event | category | flops | bytes accessed | tf_op | source)
XLA Modules:
  0.0 250.6 jit_solution(18083043665382403777)
XLA Ops:
  7.2 1.1 convert_element_type.18
  8.3 1.0 convert_element_type.8
  9.6 6.1 %collective-permute-start = (bf16[80,2048]{1,0:T(8,128)(2,1)S(1)}, bf16[80,2048]{1,0:T(8,128)(2,1)S(1)}, u32[]{:S(2)}, u32[]{:S(2)}) collective-permute-start(bf16[80,2048]{1,0:T(8,128)(2,1)S(1)} %pad_maximum_fusion), channel_id=1, source_target_pairs={{0,28},{1,29},{2,30},{3,31},{4,0},{5,1},{6,2},{7,3},{8,4},{9,5},{1... | collective-permute-start | bytes 983048 | tf_op jit(solution)/shard_map/ppermute | solution.py:16
  15.6 0.5 collective-permute-start.9
  16.4 7.3 %collective-permute-done = bf16[80,2048]{1,0:T(8,128)(2,1)S(1)} collective-permute-done((bf16[80,2048]{1,0:T(8,128)(2,1)S(1)}, bf16[80,2048]{1,0:T(8,128)(2,1)S(1)}, u32[]{:S(2)}, u32[]{:S(2)}) %collective-permute-start) | collective-permute-done | bytes 327712 | tf_op jit(solution)/shard_map/ppermute | solution.py:16
  24.2 0.4 select_reduce_fusion
  24.6 1.5 collective-permute-done.9
  26.2 7.6 %collective-permute-done.1 = bf16[80,2048]{1,0:T(8,128)(2,1)S(1)} collective-permute-done((bf16[80,2048]{1,0:T(8,128)(2,1)S(1)}, bf16[80,2048]{1,0:T(8,128)(2,1)S(1)}, u32[]{:S(2)}, u32[]{:S(2)}) %collective-permute-start.1) | collective-permute-done | bytes 327712 | tf_op jit(solution)/shard_map/ppermute | solution.py:16
  34.0 1.6 collective-permute-done.10
  35.8 8.1 %collective-permute-done.2 = bf16[80,2048]{1,0:T(8,128)(2,1)S(1)} collective-permute-done((bf16[80,2048]{1,0:T(8,128)(2,1)S(1)}, bf16[80,2048]{1,0:T(8,128)(2,1)S(1)}, u32[]{:S(2)}, u32[]{:S(2)}) %collective-permute-start.2) | collective-permute-done | bytes 327712 | tf_op jit(solution)/shard_map/ppermute | solution.py:16
  44.2 1.5 collective-permute-done.11
  45.9 9.8 %collective-permute-done.12 = bf16[80,1024]{1,0:T(8,128)(2,1)S(1)} collective-permute-done((bf16[80,1024]{1,0:T(8,128)(2,1)S(1)}, bf16[80,1024]{1,0:T(8,128)(2,1)S(1)}, u32[]{:S(2)}, u32[]{:S(2)}) %collective-permute-start.12) | collective-permute-done | bytes 163872 | tf_op jit(solution)/shard_map/ppermute | solution.py:16
  56.1 8.0 %collective-permute-done.13 = bf16[80,1024]{1,0:T(8,128)(2,1)S(1)} collective-permute-done((bf16[80,1024]{1,0:T(8,128)(2,1)S(1)}, bf16[80,1024]{1,0:T(8,128)(2,1)S(1)}, u32[]{:S(2)}, u32[]{:S(2)}) %collective-permute-start.13) | collective-permute-done | bytes 163872 | tf_op jit(solution)/shard_map/ppermute | solution.py:16
  64.4 8.1 %collective-permute-done.14 = bf16[80,1024]{1,0:T(8,128)(2,1)S(1)} collective-permute-done((bf16[80,1024]{1,0:T(8,128)(2,1)S(1)}, bf16[80,1024]{1,0:T(8,128)(2,1)S(1)}, u32[]{:S(2)}, u32[]{:S(2)}) %collective-permute-start.14) | collective-permute-done | bytes 163872 | tf_op jit(solution)/shard_map/ppermute | solution.py:16
  73.0 7.8 %collective-permute-done.15 = bf16[80,1024]{1,0:T(8,128)(2,1)S(1)} collective-permute-done((bf16[80,1024]{1,0:T(8,128)(2,1)S(1)}, bf16[80,1024]{1,0:T(8,128)(2,1)S(1)}, u32[]{:S(2)}, u32[]{:S(2)}) %collective-permute-start.15) | collective-permute-done | bytes 163872 | tf_op jit(solution)/shard_map/ppermute | solution.py:16
  80.8 3.5 %collective-permute-done.5 = bf16[80,2048]{1,0:T(8,128)(2,1)S(1)} collective-permute-done((bf16[80,2048]{1,0:T(8,128)(2,1)S(1)}, bf16[80,2048]{1,0:T(8,128)(2,1)S(1)}, u32[]{:S(2)}, u32[]{:S(2)}) %collective-permute-start.5) | collective-permute-done | bytes 327712 | tf_op jit(solution)/shard_map/ppermute | solution.py:16
  84.5 4.6 %collective-permute-done.16 = bf16[80,1024]{1,0:T(8,128)(2,1)S(1)} collective-permute-done((bf16[80,1024]{1,0:T(8,128)(2,1)S(1)}, bf16[80,1024]{1,0:T(8,128)(2,1)S(1)}, u32[]{:S(2)}, u32[]{:S(2)}) %collective-permute-start.16) | collective-permute-done | bytes 163872 | tf_op jit(solution)/shard_map/ppermute | solution.py:16
  89.4 5.0 %collective-permute-done.6 = bf16[80,2048]{1,0:T(8,128)(2,1)S(1)} collective-permute-done((bf16[80,2048]{1,0:T(8,128)(2,1)S(1)}, bf16[80,2048]{1,0:T(8,128)(2,1)S(1)}, u32[]{:S(2)}, u32[]{:S(2)}) %collective-permute-start.6) | collective-permute-done | bytes 327712 | tf_op jit(solution)/shard_map/ppermute | solution.py:16
  95.0 9.5 %collective-permute-done.7 = bf16[80,2048]{1,0:T(8,128)(2,1)S(1)} collective-permute-done((bf16[80,2048]{1,0:T(8,128)(2,1)S(1)}, bf16[80,2048]{1,0:T(8,128)(2,1)S(1)}, u32[]{:S(2)}, u32[]{:S(2)}) %collective-permute-start.7) | collective-permute-done | bytes 327712 | tf_op jit(solution)/shard_map/ppermute | solution.py:16
  105.1 9.5 %collective-permute-done.8 = bf16[80,2048]{1,0:T(8,128)(2,1)S(1)} collective-permute-done((bf16[80,2048]{1,0:T(8,128)(2,1)S(1)}, bf16[80,2048]{1,0:T(8,128)(2,1)S(1)}, u32[]{:S(2)}, u32[]{:S(2)}) %collective-permute-start.8) | collective-permute-done | bytes 327712 | tf_op jit(solution)/shard_map/ppermute | solution.py:16
  115.1 0.6 fusion.24
  115.8 2.8 %fusion.25 = f32[128,1024]{1,0:T(8,128)} fusion(f32[128,2048]{1,0:T(8,128)S(1)} %fusion.24, bf16[2048,1024]{1,0:T(8,128)(2,1)S(1)} %copy-done), kind=kOutput, calls=%fused_computation.51 | convolution fusion | flops 3221225472 | bytes 5767168 | tf_op jit(solution)/shard_map/dot_general | solution.py:64
  118.6 123.8 %all-reduce.3.cloned.1.call-done = f32[128,1024]{1,0:T(8,128)} async-done(((f32[128,1024]{1,0:T(8,128)}), f32[128,1024]{1,0:T(8,128)}) %all-reduce.3.cloned.1.call-update) | async-done | bytes 524304
  242.4 1.4 constant_dynamic-slice_fusion
  (55 shorter events, 5.2 us)
Async XLA Ops:
  7.2 9.0 %copy-start.2 = (s32[80,720]{1,0:T(8,128)S(1)}, s32[80,720]{1,0:T(8,128)}, u32[]{:S(2)}) copy-start(s32[80,720]{1,0:T(8,128)} %param.8) | copy-start | bytes 691204
  7.2 16.8 %copy-start.3 = (f32[80,16]{0,1:T(8,128)S(1)}, f32[80,16]{0,1:T(8,128)}, u32[]{:S(2)}) copy-start(f32[80,16]{0,1:T(8,128)} %param.10) | copy-start | bytes 15364
  7.2 16.9 %copy-start.4 = (s32[80,16]{0,1:T(8,128)S(1)}, s32[80,16]{0,1:T(8,128)}, u32[]{:S(2)}) copy-start(s32[80,16]{0,1:T(8,128)} %param.9) | copy-start | bytes 15364
  7.2 235.2 %all-reduce.3.cloned.1.call-start = ((), (), s32[]{:S(2)}) async-start(), calls=%async_computation | async-start | bytes 1048576
  9.6 14.2 %collective-permute-start = (bf16[80,2048]{1,0:T(8,128)(2,1)S(1)}, bf16[80,2048]{1,0:T(8,128)(2,1)S(1)}, u32[]{:S(2)}, u32[]{:S(2)}) collective-permute-start(bf16[80,2048]{1,0:T(8,128)(2,1)S(1)} %pad_maximum_fusion), channel_id=1, source_target_pairs={{0,28},{1,29},{2,30},{3,31},{4,0},{5,1},{6,2},{7,3},{8,4},{9,5},{1... | collective-permute-start | bytes 983048 | tf_op jit(solution)/shard_map/ppermute | solution.py:16
  15.6 10.5 %collective-permute-start.9 = (bf16[80,1024]{1,0:T(8,128)(2,1)S(1)}, bf16[80,1024]{1,0:T(8,128)(2,1)S(1)}, u32[]{:S(2)}, u32[]{:S(2)}) collective-permute-start(bf16[80,1024]{1,0:T(8,128)(2,1)S(1)} %get-tuple-element.6), channel_id=1, source_target_pairs={{0,28},{1,29},{2,30},{3,31},{4,0},{5,1},{6,2},{7,3},{8,4},{9,5},{1... | collective-permute-start | bytes 491528 | tf_op jit(solution)/shard_map/ppermute | solution.py:16
  23.7 10.1 %collective-permute-start.1 = (bf16[80,2048]{1,0:T(8,128)(2,1)S(1)}, bf16[80,2048]{1,0:T(8,128)(2,1)S(1)}, u32[]{:S(2)}, u32[]{:S(2)}) collective-permute-start(bf16[80,2048]{1,0:T(8,128)(2,1)S(1)} %collective-permute-done), channel_id=1, source_target_pairs={{0,1},{1,2},{2,3},{3,4},{4,5},{5,6},{6,7},{7,8},{8,9},{9,10},{10,1... | collective-permute-start | bytes 983048 | tf_op jit(solution)/shard_map/ppermute | solution.py:16
  26.1 9.5 %collective-permute-start.10 = (bf16[80,1024]{1,0:T(8,128)(2,1)S(1)}, bf16[80,1024]{1,0:T(8,128)(2,1)S(1)}, u32[]{:S(2)}, u32[]{:S(2)}) collective-permute-start(bf16[80,1024]{1,0:T(8,128)(2,1)S(1)} %collective-permute-done.9), channel_id=1, source_target_pairs={{0,1},{1,2},{2,3},{3,4},{4,5},{5,6},{6,7},{7,8},{8,9},{9,10},{10,1... | collective-permute-start | bytes 491528 | tf_op jit(solution)/shard_map/ppermute | solution.py:16
  33.8 10.1 %collective-permute-start.2 = (bf16[80,2048]{1,0:T(8,128)(2,1)S(1)}, bf16[80,2048]{1,0:T(8,128)(2,1)S(1)}, u32[]{:S(2)}, u32[]{:S(2)}) collective-permute-start(bf16[80,2048]{1,0:T(8,128)(2,1)S(1)} %collective-permute-done.1), channel_id=1, source_target_pairs={{0,1},{1,2},{2,3},{3,4},{4,5},{5,6},{6,7},{7,8},{8,9},{9,10},{10,1... | collective-permute-start | bytes 983048 | tf_op jit(solution)/shard_map/ppermute | solution.py:16
  35.6 10.1 %collective-permute-start.11 = (bf16[80,1024]{1,0:T(8,128)(2,1)S(1)}, bf16[80,1024]{1,0:T(8,128)(2,1)S(1)}, u32[]{:S(2)}, u32[]{:S(2)}) collective-permute-start(bf16[80,1024]{1,0:T(8,128)(2,1)S(1)} %collective-permute-done.10), channel_id=1, source_target_pairs={{0,1},{1,2},{2,3},{3,4},{4,5},{5,6},{6,7},{7,8},{8,9},{9,10},{10,1... | collective-permute-start | bytes 491528 | tf_op jit(solution)/shard_map/ppermute | solution.py:16
  43.9 11.9 %collective-permute-start.3 = (bf16[80,2048]{1,0:T(8,128)(2,1)S(1)}, bf16[80,2048]{1,0:T(8,128)(2,1)S(1)}, u32[]{:S(2)}, u32[]{:S(2)}) collective-permute-start(bf16[80,2048]{1,0:T(8,128)(2,1)S(1)} %collective-permute-done.2), channel_id=1, source_target_pairs={{0,1},{1,2},{2,3},{3,4},{4,5},{5,6},{6,7},{7,8},{8,9},{9,10},{10,1... | collective-permute-start | bytes 983048 | tf_op jit(solution)/shard_map/ppermute | solution.py:16
  45.7 10.1 %collective-permute-start.12 = (bf16[80,1024]{1,0:T(8,128)(2,1)S(1)}, bf16[80,1024]{1,0:T(8,128)(2,1)S(1)}, u32[]{:S(2)}, u32[]{:S(2)}) collective-permute-start(bf16[80,1024]{1,0:T(8,128)(2,1)S(1)} %collective-permute-done.11), channel_id=1, source_target_pairs={{0,1},{1,2},{2,3},{3,4},{4,5},{5,6},{6,7},{7,8},{8,9},{9,10},{10,1... | collective-permute-start | bytes 491528 | tf_op jit(solution)/shard_map/ppermute | solution.py:16
  55.8 8.3 %collective-permute-start.13 = (bf16[80,1024]{1,0:T(8,128)(2,1)S(1)}, bf16[80,1024]{1,0:T(8,128)(2,1)S(1)}, u32[]{:S(2)}, u32[]{:S(2)}) collective-permute-start(bf16[80,1024]{1,0:T(8,128)(2,1)S(1)} %collective-permute-done.12), channel_id=1, source_target_pairs={{0,1},{1,2},{2,3},{3,4},{4,5},{5,6},{6,7},{7,8},{8,9},{9,10},{10,1... | collective-permute-start | bytes 491528 | tf_op jit(solution)/shard_map/ppermute | solution.py:16
  55.8 16.7 %collective-permute-start.4 = (bf16[80,2048]{1,0:T(8,128)(2,1)S(1)}, bf16[80,2048]{1,0:T(8,128)(2,1)S(1)}, u32[]{:S(2)}, u32[]{:S(2)}) collective-permute-start(bf16[80,2048]{1,0:T(8,128)(2,1)S(1)} %collective-permute-done.3), channel_id=1, source_target_pairs={{0,1},{1,2},{2,3},{3,4},{4,5},{5,6},{6,7},{7,8},{8,9},{9,10},{10,1... | collective-permute-start | bytes 983048 | tf_op jit(solution)/shard_map/ppermute | solution.py:16
  64.1 8.3 %collective-permute-start.14 = (bf16[80,1024]{1,0:T(8,128)(2,1)S(1)}, bf16[80,1024]{1,0:T(8,128)(2,1)S(1)}, u32[]{:S(2)}, u32[]{:S(2)}) collective-permute-start(bf16[80,1024]{1,0:T(8,128)(2,1)S(1)} %collective-permute-done.13), channel_id=1, source_target_pairs={{0,1},{1,2},{2,3},{3,4},{4,5},{5,6},{6,7},{7,8},{8,9},{9,10},{10,1... | collective-permute-start | bytes 491528 | tf_op jit(solution)/shard_map/ppermute | solution.py:16
  72.5 8.3 %collective-permute-start.15 = (bf16[80,1024]{1,0:T(8,128)(2,1)S(1)}, bf16[80,1024]{1,0:T(8,128)(2,1)S(1)}, u32[]{:S(2)}, u32[]{:S(2)}) collective-permute-start(bf16[80,1024]{1,0:T(8,128)(2,1)S(1)} %collective-permute-done.14), channel_id=1, source_target_pairs={{0,1},{1,2},{2,3},{3,4},{4,5},{5,6},{6,7},{7,8},{8,9},{9,10},{10,1... | collective-permute-start | bytes 491528 | tf_op jit(solution)/shard_map/ppermute | solution.py:16
  72.5 11.8 %collective-permute-start.5 = (bf16[80,2048]{1,0:T(8,128)(2,1)S(1)}, bf16[80,2048]{1,0:T(8,128)(2,1)S(1)}, u32[]{:S(2)}, u32[]{:S(2)}) collective-permute-start(bf16[80,2048]{1,0:T(8,128)(2,1)S(1)} %collective-permute-done.4), channel_id=1, source_target_pairs={{0,1},{1,2},{2,3},{3,4},{4,5},{5,6},{6,7},{7,8},{8,9},{9,10},{10,1... | collective-permute-start | bytes 983048 | tf_op jit(solution)/shard_map/ppermute | solution.py:16
  80.8 8.3 %collective-permute-start.16 = (bf16[80,1024]{1,0:T(8,128)(2,1)S(1)}, bf16[80,1024]{1,0:T(8,128)(2,1)S(1)}, u32[]{:S(2)}, u32[]{:S(2)}) collective-permute-start(bf16[80,1024]{1,0:T(8,128)(2,1)S(1)} %collective-permute-done.15), channel_id=1, source_target_pairs={{0,1},{1,2},{2,3},{3,4},{4,5},{5,6},{6,7},{7,8},{8,9},{9,10},{10,1... | collective-permute-start | bytes 491528 | tf_op jit(solution)/shard_map/ppermute | solution.py:16
  84.3 10.1 %collective-permute-start.6 = (bf16[80,2048]{1,0:T(8,128)(2,1)S(1)}, bf16[80,2048]{1,0:T(8,128)(2,1)S(1)}, u32[]{:S(2)}, u32[]{:S(2)}) collective-permute-start(bf16[80,2048]{1,0:T(8,128)(2,1)S(1)} %collective-permute-done.5), channel_id=1, source_target_pairs={{0,1},{1,2},{2,3},{3,4},{4,5},{5,6},{6,7},{7,8},{8,9},{9,10},{10,1... | collective-permute-start | bytes 983048 | tf_op jit(solution)/shard_map/ppermute | solution.py:16
  89.1 25.7 %collective-permute-start.17 = (bf16[80,1024]{1,0:T(8,128)(2,1)S(1)}, bf16[80,1024]{1,0:T(8,128)(2,1)S(1)}, u32[]{:S(2)}, u32[]{:S(2)}) collective-permute-start(bf16[80,1024]{1,0:T(8,128)(2,1)S(1)} %collective-permute-done.16), channel_id=1, source_target_pairs={{0,1},{1,2},{2,3},{3,4},{4,5},{5,6},{6,7},{7,8},{8,9},{9,10},{10,1... | collective-permute-start | bytes 491528 | tf_op jit(solution)/shard_map/ppermute | solution.py:16
  94.4 10.1 %collective-permute-start.7 = (bf16[80,2048]{1,0:T(8,128)(2,1)S(1)}, bf16[80,2048]{1,0:T(8,128)(2,1)S(1)}, u32[]{:S(2)}, u32[]{:S(2)}) collective-permute-start(bf16[80,2048]{1,0:T(8,128)(2,1)S(1)} %collective-permute-done.6), channel_id=1, source_target_pairs={{0,1},{1,2},{2,3},{3,4},{4,5},{5,6},{6,7},{7,8},{8,9},{9,10},{10,1... | collective-permute-start | bytes 983048 | tf_op jit(solution)/shard_map/ppermute | solution.py:16
  95.0 20.8 %copy-start = (bf16[2048,1024]{1,0:T(8,128)(2,1)S(1)}, bf16[2048,1024]{1,0:T(8,128)(2,1)}, u32[]{:S(2)}) copy-start(bf16[2048,1024]{1,0:T(8,128)(2,1)} %param.11) | copy-start | bytes 12582916
  104.5 10.1 %collective-permute-start.8 = (bf16[80,2048]{1,0:T(8,128)(2,1)S(1)}, bf16[80,2048]{1,0:T(8,128)(2,1)S(1)}, u32[]{:S(2)}, u32[]{:S(2)}) collective-permute-start(bf16[80,2048]{1,0:T(8,128)(2,1)S(1)} %collective-permute-done.7), channel_id=1, source_target_pairs={{0,1},{1,2},{2,3},{3,4},{4,5},{5,6},{6,7},{7,8},{8,9},{9,10},{10,1... | collective-permute-start | bytes 983048 | tf_op jit(solution)/shard_map/ppermute | solution.py:16
  115.1 128.7 %copy-start.1 = (bf16[80,2048]{1,0:T(8,128)(2,1)}, bf16[80,2048]{1,0:T(8,128)(2,1)S(1)}, u32[]{:S(2)}) copy-start(bf16[80,2048]{1,0:T(8,128)(2,1)S(1)} %pad_maximum_fusion.1) | copy-start | bytes 983044
Sparse Core Ops, SparseCore 0:
  118.7 123.6 all-reduce.2
where the time goes:
time: 251 us
  waiting for transfers between devices  217 us (86%)
  between operations  14.3 us (6%)
  matrix products  7.89 us (3%)
  starting transfers between devices  6.8 us (3%)
  other arithmetic  2.74 us (1%)
    unnamed x2, waiting for transfers between devices  124 us
    ppermute x18, waiting for transfers between devices, passed_along(): return lax.ppermute(value, axis, pairs)  93.5 us
    ppermute x18, starting transfers between devices, passed_along(): return lax.ppermute(value, axis, pairs)  6.76 us
  transfers between devices with their start and end apart: 19, of which 16 were waited for; matrix products, arithmetic and copies ran while one was open for 2% of the time, Pallas kernels for 0%

commit v1 on v0

v1 whole, which is shorter than its diff:
```python
import functools

import jax
import jax.numpy as jnp
from jax import lax
from jax.experimental import pallas as pl
from jax.experimental.pallas import tpu as pltpu
from jax.sharding import PartitionSpec as P

C = 80
F = 1024
TT = 4
WIN = 9
CT = 1024
Q = 4
FC = F // Q
MB = 4
MESH = pl.DeviceIdType.MESH

X, Y, Z, V, T, PEER = 0, 1, 2, 3, 4, 5
KINDS = 9
TRANSIT = WIN


def body(
    n, rec, grn, mask, lists, weights, tg_hbm, adj_out, ker_out,
    buf, mask_bf, tg, w_acc, terms, halves, wide, packed, landed,
    send_sem, recv_sem, tg_sem, half_sem, sum_sem,
):
    chips = n // 2
    planes = n // 8
    half = TT * chips
    me = lax.axis_index("sta")
    core = lax.rem(me, 2)
    chip = me // 2
    j = lax.rem(chip, 4)
    plane = me // 8
    odd = lax.rem(j, 2)
    upper = j // 2
    inner = lax.rem((j + 1) // 2, 2)
    peer = me + 1 - 2 * core
    x_dev = me + 2 - 4 * odd
    y_dev = me + 4 - 8 * upper
    z_dev = lax.rem(plane + 1 - 2 * upper + planes, planes) * 8 + lax.rem(me, 8)
    slot_x = 6 - 4 * odd
    slot_v = 2 + 4 * odd
    slot_y = 8 - 8 * upper
    slot_z = 8 * upper
    is0 = core == 0
    is1 = core == 1

    barrier = pltpu.get_barrier_semaphore()
    pl.semaphore_signal(barrier, inc=1, device_id=(peer,), device_id_type=MESH)

    @pl.loop(1, chips)
    def _(o):
        other = lax.rem(chip + o, chips) * 2 + core
        pl.semaphore_signal(barrier, inc=1, device_id=(other,), device_id_type=MESH)

    tg_copy = pltpu.make_async_copy(tg_hbm, tg, tg_sem)
    tg_copy.start()

    def part(ref, q, imag):
        return ref[:, imag * F + q * FC : imag * F + (q + 1) * FC].astype(jnp.float32)

    def fill(q):
        dr, di = part(rec, q, 0), part(rec, q, 1)
        gr, gi = part(grn, q, 0), part(grn, q, 1)
        buf[q, 4, :, 0:FC] = (dr * gr + di * gi).astype(jnp.bfloat16)
        buf[q, 4, :, FC : 2 * FC] = (dr * gi - di * gr).astype(jnp.bfloat16)
        buf[q, 4, :, 2 * FC : 3 * FC] = (gr * gr + gi * gi).astype(jnp.bfloat16)

    def move(q, src, dst, sender, kind, device):
        return pltpu.make_async_remote_copy(
            src_ref=buf.at[q, src], dst_ref=buf.at[q, dst],
            send_sem=send_sem.at[q, sender], recv_sem=recv_sem.at[q, kind],
            device_id=(device,), device_id_type=MESH,
        )

    def relay(q, src, which):
        return move(q, src, src + 2 * core - 1, PEER + which, PEER + which, peer)

    def arrived(q, slot, kind):
        move(q, slot, slot, kind, kind, peer).wait_recv()

    def sent(q, kind):
        move(q, 4, 4, kind, kind, peer).wait_send()

    def send_own(q):
        move(q, 4, slot_z, Y, Y, y_dev).start()
        move(q, 4, slot_v, X, X, x_dev).start()
        relay(q, 4, 0).start()

    def stage1(q):
        arrived(q, slot_y, Y)
        move(q, slot_y, slot_z, Z, Z, z_dev).start()

        @pl.when(core == upper)
        def _():
            relay(q, slot_y, 3).start()

        @pl.when(is0 & (inner == 0))
        def _():
            move(q, slot_y, slot_x, V, V, x_dev).start()

        arrived(q, slot_x, X)

        @pl.when(is1 & (inner == 0))
        def _():
            move(q, slot_x, slot_v, V, V, y_dev).start()

        @pl.when(is1 & (inner == 1))
        def _():
            move(q, slot_x, TRANSIT, V, T, y_dev).start()

        relay(q, slot_x, 1).start()

    def stage2(q):
        @pl.when(is1 & (inner == 0))
        def _():
            arrived(q, TRANSIT, T)
            move(q, TRANSIT, slot_v, T, V, z_dev).start()

        arrived(q, slot_z, Z)

        @pl.when(is0 & (inner == 1))
        def _():
            move(q, slot_z, slot_x, V, V, x_dev).start()

        @pl.when(core != upper)
        def _():
            relay(q, slot_z, 3).start()

    def stage3(q):
        arrived(q, slot_v, V)
        relay(q, slot_v, 2).start()

    def peer_slot(slot):
        return slot + 1 - 2 * core

    def stage4(q):
        arrived(q, peer_slot(4), PEER)
        arrived(q, peer_slot(slot_x), PEER + 1)
        arrived(q, peer_slot(slot_v), PEER + 2)
        theirs = 8 * core
        arrived(q, peer_slot(theirs), PEER + 3)
        window = buf[q, 0:WIN].reshape(WIN * C, 3 * FC)
        sums = jnp.dot(mask_bf[...], window, preferred_element_type=jnp.float32)
        sums = sums * (1.0 / jnp.sqrt(jnp.float32(WIN * C)))
        q_real, q_imag, p = sums[:, :FC], sums[:, FC : 2 * FC], sums[:, 2 * FC :]
        dr, di = part(rec, q, 0), part(rec, q, 1)
        gr, gi = part(grn, q, 0), part(grn, q, 1)
        real = (dr * q_real - di * q_imag - gr * p).astype(jnp.bfloat16)
        imag = (dr * q_imag + di * q_real - gi * p).astype(jnp.bfloat16)
        adj_out[:, q * FC : (q + 1) * FC] = real
        adj_out[:, F + q * FC : F + (q + 1) * FC] = imag
        if q == 0:
            tg_copy.wait()
        more = jnp.dot(
            real, tg[q * FC : (q + 1) * FC, :], preferred_element_type=jnp.float32
        ) + jnp.dot(
            imag, tg[F + q * FC : F + (q + 1) * FC, :], preferred_element_type=jnp.float32
        )
        w_acc[...] = more if q == 0 else w_acc[...] + more

    fill(0)
    pl.semaphore_wait(barrier, chips)
    send_own(0)
    for q in range(1, Q):
        fill(q)
        send_own(q)

    mask_bf[...] = mask[...].astype(jnp.float32).astype(jnp.bfloat16)
    row = lax.broadcasted_iota(jnp.int32, (2 * half, C), 0)
    late = jnp.where(row >= half, 1, 0)
    rest = row - half * late
    tile = (rest >> 2) * (2 * TT) + late * TT + (rest & 3)
    tile_map = jnp.zeros((2 * half, C), jnp.float32)
    for l in range(lists.shape[0]):
        tile_map = tile_map + jnp.where(lists[l : l + 1, :] == tile, weights[l : l + 1, :], 0.0)
    map_high = tile_map.astype(jnp.bfloat16)
    map_low = (tile_map - map_high.astype(jnp.float32)).astype(jnp.bfloat16)

    for step in range(Q + 3):
        if step < Q:
            stage1(step)
        if 0 <= step - 1 < Q:
            stage2(step - 1)
        if 0 <= step - 2 < Q:
            stage3(step - 2)
        if 0 <= step - 3 < Q:
            stage4(step - 3)

    w = w_acc[...]
    w_high = w.astype(jnp.bfloat16)
    w_low = (w - w_high.astype(jnp.float32)).astype(jnp.bfloat16)
    terms[...] = (
        jnp.dot(map_high, w_high, preferred_element_type=jnp.float32)
        + jnp.dot(map_high, w_low, preferred_element_type=jnp.float32)
        + jnp.dot(map_low, w_high, preferred_element_type=jnp.float32)
    )
    to_peer = pltpu.make_async_remote_copy(
        src_ref=terms.at[pl.ds(pl.multiple_of((1 - core) * half, half), half)], dst_ref=halves,
        send_sem=half_sem.at[0], recv_sem=half_sem.at[1],
        device_id=(peer,), device_id_type=MESH,
    )
    to_peer.start()
    to_peer.wait_recv()
    width = CT // MB

    @pl.loop(0, chips // 2)
    def _(i):
        start = pl.multiple_of(8 * i, 8)
        both = terms[pl.ds(pl.multiple_of(core * half + start, 8), 8), :] + halves[pl.ds(start, 8), :]
        for m in range(MB):
            cols = both[:, m * width : (m + 1) * width]
            wide[2 * i, m * TT : (m + 1) * TT, :] = cols[0:TT]
            wide[2 * i + 1, m * TT : (m + 1) * TT, :] = cols[TT : 2 * TT]
        packed[2 * i] = wide[2 * i].astype(jnp.bfloat16)
        packed[2 * i + 1] = wide[2 * i + 1].astype(jnp.bfloat16)

    def piece(o):
        other = lax.rem(chip + o, chips)
        return pltpu.make_async_remote_copy(
            src_ref=packed.at[other], dst_ref=landed.at[o - 1],
            send_sem=sum_sem.at[0], recv_sem=sum_sem.at[1],
            device_id=(other * 2 + core,), device_id_type=MESH,
        )

    @pl.loop(1, chips)
    def _(o):
        piece(o).start()

    for q in range(Q):
        sent(q, X)
        sent(q, Y)
        sent(q, Z)
        for which in range(4):
            sent(q, PEER + which)

        sent(q, V)

        @pl.when(is1 & (inner == 0))
        def _():
            sent(q, T)

    to_peer.wait_send()
    everything = pltpu.make_async_remote_copy(
        src_ref=packed.at[0 : chips - 1], dst_ref=landed,
        send_sem=sum_sem.at[0], recv_sem=sum_sem.at[1],
        device_id=(peer,), device_id_type=MESH,
    )
    everything.wait_recv()
    total = lax.fori_loop(
        0, chips - 1, lambda o, t: t + landed[o].astype(jnp.float32), wide[chip]
    )
    for m in range(MB):
        ker_out[:, m * width : (m + 1) * width] = total[m * TT : (m + 1) * TT]
    everything.wait_send()


def local(n, records, green, pair_mask, tile_lists, tile_weights, tile_green):
    chips = n // 2
    half = TT * chips
    vmem = pl.BlockSpec(memory_space=pltpu.VMEM)
    return pl.pallas_call(
        functools.partial(body, n),
        out_shape=(
            jax.ShapeDtypeStruct((C, 2 * F), jnp.bfloat16),
            jax.ShapeDtypeStruct((TT, CT), jnp.float32),
        ),
        in_specs=[vmem] * 5 + [pl.BlockSpec(memory_space=pl.ANY)],
        out_specs=(vmem, vmem),
        scratch_shapes=[
            pltpu.VMEM((Q, WIN + 1, C, 3 * FC), jnp.bfloat16),
            pltpu.VMEM((C, WIN * C), jnp.bfloat16),
            pltpu.VMEM((2 * F, CT), jnp.bfloat16),
            pltpu.VMEM((C, CT), jnp.float32),
            pltpu.VMEM((2 * half, CT), jnp.float32),
            pltpu.VMEM((half, CT), jnp.float32),
            pltpu.VMEM((chips, MB * TT, CT // MB), jnp.float32),
            pltpu.VMEM((chips, MB * TT, CT // MB), jnp.bfloat16),
            pltpu.VMEM((chips - 1, MB * TT, CT // MB), jnp.bfloat16),
            pltpu.SemaphoreType.DMA((Q, KINDS)),
            pltpu.SemaphoreType.DMA((Q, KINDS)),
            pltpu.SemaphoreType.DMA,
            pltpu.SemaphoreType.DMA((2,)),
            pltpu.SemaphoreType.DMA((2,)),
        ],
        compiler_params=pltpu.CompilerParams(
            collective_id=0, has_side_effects=True, vmem_limit_bytes=44 * 2**20
        ),
        cost_estimate=pl.CostEstimate(flops=10**9, bytes_accessed=6 * 10**6, transcendentals=0),
    )(records, green, pair_mask, tile_lists.T, tile_weights.T, tile_green)


def solution(mesh):
    n = mesh.shape["sta"]
    return jax.shard_map(
        functools.partial(local, n),
        mesh=mesh,
        in_specs=(P("sta", None),) * 6,
        out_specs=(P("sta", None), P("sta", None)),
        check_vma=False,
    )
```

time: 251 us -> 48.6 us (0.19)
  waiting for transfers between devices: 217 us -> 0 us
  Pallas kernels: 0 us -> 39.9 us
  between operations: 14.3 us -> 0.65 us
  matrix products: 7.89 us -> 0 us
  starting transfers between devices: 6.8 us -> 0 us
  local copies, waits for them, and re-layouts: 1.57 us -> 7.79 us
  other arithmetic: 2.74 us -> 0 us
    unnamed x2 -> x0, waiting for transfers between devices: 124 us -> none
    ppermute x18 -> x0, waiting for transfers between devices: 93.5 us -> none  [passed_along(): return lax.ppermute(value, axis, pairs)]
    pallas_call x0 -> x1, Pallas kernels: none -> 39.9 us  [local(): pl.pallas_call(functools.partial(body, n), out_shape=(jax.ShapeDtypeStruc...]
    dot_general x20 -> x0, matrix products: 7.89 us -> none  [the longest x1 2.78 us: local(): jnp.dot(spread, green_wide, precision=lax.Precision.HIGHEST)]
    ppermute x18 -> x0, starting transfers between devices: 6.76 us -> none  [passed_along(): return lax.ppermute(value, axis, pairs)]
    unnamed x13 -> x14, local copies, waits for them, and re-layouts: 1.57 us -> 7.79 us
  transfers between devices with their start and end apart: 19 -> 0, of which waited for: 16 -> 0; matrix products, arithmetic and copies ran while one was open for 2% -> 0% of each run, Pallas kernels for 0% -> 0%
where the time goes in v1:
time: 48.6 us; the launch traced here: 48.3 us
  Pallas kernels  39.9 us (82%)
  local copies, waits for them, and re-layouts  7.79 us (16%)
  between operations  0.65 us (1%)
    pallas_call x1, Pallas kernels, local(): pl.pallas_call(functools.partial(body, n), out_shape=(jax.ShapeDtypeStruc...  39.9 us
    unnamed x14, local copies, waits for them, and re-layouts  7.79 us

profile of v1, /device:TPU:0, one launch (start us, length us, event | category | flops | bytes accessed | tf_op | source)
XLA Modules:
  0.0 48.3 jit_solution(17632074242760052266)
XLA Ops:
  0.6 0.0 copy-start
  0.6 2.2 %copy-done = bf16[2048,1024]{1,0:T(8,128)(2,1)S(1)} copy-done((bf16[2048,1024]{1,0:T(8,128)(2,1)S(1)}, bf16[2048,1024]{1,0:T(8,128)(2,1)}, u32[]{:S(2)}) %copy-start) | copy-done | bytes 4194328
  2.8 0.0 copy-start.1
  2.8 1.0 %copy-done.1 = bf16[80,2048]{1,0:T(8,128)(2,1)S(1)} copy-done((bf16[80,2048]{1,0:T(8,128)(2,1)S(1)}, bf16[80,2048]{1,0:T(8,128)(2,1)}, u32[]{:S(2)}) %copy-start.1) | copy-done | bytes 327704
  3.8 0.0 copy-start.2
  3.8 1.0 %copy-done.2 = bf16[80,2048]{1,0:T(8,128)(2,1)S(1)} copy-done((bf16[80,2048]{1,0:T(8,128)(2,1)S(1)}, bf16[80,2048]{1,0:T(8,128)(2,1)}, u32[]{:S(2)}) %copy-start.2) | copy-done | bytes 327704
  4.8 0.0 copy-start.3
  4.8 0.9 %copy-done.3 = s32[80,720]{1,0:T(8,128)S(1)} copy-done((s32[80,720]{1,0:T(8,128)S(1)}, s32[80,720]{1,0:T(8,128)}, u32[]{:S(2)}) %copy-start.3) | copy-done | bytes 230424
  5.7 0.0 copy-start.4
  5.7 0.7 %copy-done.4 = s32[80,16]{0,1:T(8,128)S(1)} copy-done((s32[80,16]{0,1:T(8,128)S(1)}, s32[80,16]{0,1:T(8,128)}, u32[]{:S(2)}) %copy-start.4) | copy-done | bytes 5144
  6.4 0.0 copy-start.5
  6.4 0.7 %copy-done.5 = f32[80,16]{0,1:T(8,128)S(1)} copy-done((f32[80,16]{0,1:T(8,128)S(1)}, f32[80,16]{0,1:T(8,128)}, u32[]{:S(2)}) %copy-start.5) | copy-done | bytes 5144
  7.1 39.9 %shard_map.77 = (bf16[80,2048]{1,0:T(8,128)(2,1)S(1)}, f32[4,1024]{1,0:T(4,128)S(1)}) custom-call(bf16[80,2048]{1,0:T(8,128)(2,1)S(1)} %copy-done.1, bf16[80,2048]{1,0:T(8,128)(2,1)S(1)} %copy-done.2, s32[80,720]{1,0:T(8,128)S(1)} %copy-done.3, s32[16,80]{1,0:T(8,128)S(1)} %bitcast.2, f32[16,80]{1,0:T(8,128)S(1)} %bitcast.3, bf16[2048,1024]{1,0:T(8,128)(2,1)S(1)} %copy-done), custom_call_target="tpu_custom_call" | custom-call | flops 1000000000 | bytes 6000000 | tf_op jit(solution)/shard_map/pallas_call | solution.py:266
  47.0 0.7 %copy.10 = bf16[80,2048]{1,0:T(8,128)(2,1)} copy(bf16[80,2048]{1,0:T(8,128)(2,1)S(1)} %get-tuple-element.4) | data formatting | bytes 655360
  47.7 0.6 %copy.11 = f32[4,1024]{1,0:T(4,128)} copy(f32[4,1024]{1,0:T(4,128)S(1)} %get-tuple-element.5) | data formatting | bytes 32768
Async XLA Ops:
  0.6 2.2 %copy-start = (bf16[2048,1024]{1,0:T(8,128)(2,1)S(1)}, bf16[2048,1024]{1,0:T(8,128)(2,1)}, u32[]{:S(2)}) copy-start(bf16[2048,1024]{1,0:T(8,128)(2,1)} %tg_hbm.1) | copy-start | bytes 12582916
  2.8 1.0 %copy-start.1 = (bf16[80,2048]{1,0:T(8,128)(2,1)S(1)}, bf16[80,2048]{1,0:T(8,128)(2,1)}, u32[]{:S(2)}) copy-start(bf16[80,2048]{1,0:T(8,128)(2,1)} %rec.1) | copy-start | bytes 983044
  3.8 1.0 %copy-start.2 = (bf16[80,2048]{1,0:T(8,128)(2,1)S(1)}, bf16[80,2048]{1,0:T(8,128)(2,1)}, u32[]{:S(2)}) copy-start(bf16[80,2048]{1,0:T(8,128)(2,1)} %grn.1) | copy-start | bytes 983044
  4.8 0.9 %copy-start.3 = (s32[80,720]{1,0:T(8,128)S(1)}, s32[80,720]{1,0:T(8,128)}, u32[]{:S(2)}) copy-start(s32[80,720]{1,0:T(8,128)} %mask.1) | copy-start | bytes 691204
  5.7 0.7 %copy-start.4 = (s32[80,16]{0,1:T(8,128)S(1)}, s32[80,16]{0,1:T(8,128)}, u32[]{:S(2)}) copy-start(s32[80,16]{0,1:T(8,128)} %param.9) | copy-start | bytes 15364
  6.4 0.7 %copy-start.5 = (f32[80,16]{0,1:T(8,128)S(1)}, f32[80,16]{0,1:T(8,128)}, u32[]{:S(2)}) copy-start(f32[80,16]{0,1:T(8,128)} %param.10) | copy-start | bytes 15364

commit v2 on v1

--- a/solution.py
+++ b/solution.py
@@ -12,8 +12,9 @@
 TT = 4
 WIN = 9
 CT = 1024
-Q = 4
+Q = 8
 FC = F // Q
+AHEAD = 2
 MB = 4
 MESH = pl.DeviceIdType.MESH
 
@@ -23,9 +24,9 @@
 
 
 def body(
-    n, rec, grn, mask, lists, weights, tg_hbm, adj_out, ker_out,
-    buf, mask_bf, tg, w_acc, terms, halves, wide, packed, landed,
-    send_sem, recv_sem, tg_sem, half_sem, sum_sem,
+    n, rec_hbm, grn_hbm, mask_hbm, lists_hbm, weights_hbm, tg_hbm, adj_hbm, ker_out,
+    adj_out, rec, grn, mask, lists, weights, buf, mask_bf, map_all, tg, w_acc, terms, halves, wide, packed, landed,
+    send_sem, recv_sem, in_sem, half_sem, sum_sem,
 ):
     chips = n // 2
     planes = n // 8
@@ -49,6 +50,17 @@
     is0 = core == 0
     is1 = core == 1
 
+    fetches = [
+        pltpu.make_async_copy(src, dst, in_sem.at[i])
+        for i, (src, dst) in enumerate(
+            (
+                (rec_hbm, rec), (grn_hbm, grn), (mask_hbm, mask),
+                (lists_hbm, lists), (weights_hbm, weights), (tg_hbm, tg),
+            )
+        )
+    ]
+    fetches[0].start()
+    fetches[1].start()
     barrier = pltpu.get_barrier_semaphore()
     pl.semaphore_signal(barrier, inc=1, device_id=(peer,), device_id_type=MESH)
 
@@ -57,8 +69,8 @@
         other = lax.rem(chip + o, chips) * 2 + core
         pl.semaphore_signal(barrier, inc=1, device_id=(other,), device_id_type=MESH)
 
-    tg_copy = pltpu.make_async_copy(tg_hbm, tg, tg_sem)
-    tg_copy.start()
+    for fetch in fetches[2:]:
+        fetch.start()
 
     def part(ref, q, imag):
         return ref[:, imag * F + q * FC : imag * F + (q + 1) * FC].astype(jnp.float32)
@@ -155,7 +167,7 @@
         adj_out[:, q * FC : (q + 1) * FC] = real
         adj_out[:, F + q * FC : F + (q + 1) * FC] = imag
         if q == 0:
-            tg_copy.wait()
+            fetches[5].wait()
         more = jnp.dot(
             real, tg[q * FC : (q + 1) * FC, :], preferred_element_type=jnp.float32
         ) + jnp.dot(
@@ -163,13 +175,18 @@
         )
         w_acc[...] = more if q == 0 else w_acc[...] + more
 
+    fetches[0].wait()
+    fetches[1].wait()
     fill(0)
     pl.semaphore_wait(barrier, chips)
     send_own(0)
     for q in range(1, Q):
         fill(q)
-        send_own(q)
-
+        if q < AHEAD:
+            send_own(q)
+
+    for fetch in fetches[2:5]:
+        fetch.wait()
     mask_bf[...] = mask[...].astype(jnp.float32).astype(jnp.bfloat16)
     row = lax.broadcasted_iota(jnp.int32, (2 * half, C), 0)
     late = jnp.where(row >= half, 1, 0)
@@ -180,10 +197,13 @@
         tile_map = tile_map + jnp.where(lists[l : l + 1, :] == tile, weights[l : l + 1, :], 0.0)
     map_high = tile_map.astype(jnp.bfloat16)
     map_low = (tile_map - map_high.astype(jnp.float32)).astype(jnp.bfloat16)
+    map_all[...] = jnp.concatenate([map_high, map_high, map_low], axis=1)
 
     for step in range(Q + 3):
         if step < Q:
             stage1(step)
+        if step + AHEAD < Q:
+            send_own(step + AHEAD)
         if 0 <= step - 1 < Q:
             stage2(step - 1)
         if 0 <= step - 2 < Q:
@@ -191,14 +211,14 @@
         if 0 <= step - 3 < Q:
             stage4(step - 3)
 
+    adj_copy = pltpu.make_async_copy(adj_out, adj_hbm, in_sem.at[6])
+    adj_copy.start()
+
     w = w_acc[...]
     w_high = w.astype(jnp.bfloat16)
     w_low = (w - w_high.astype(jnp.float32)).astype(jnp.bfloat16)
-    terms[...] = (
-        jnp.dot(map_high, w_high, preferred_element_type=jnp.float32)
-        + jnp.dot(map_high, w_low, preferred_element_type=jnp.float32)
-        + jnp.dot(map_low, w_high, preferred_element_type=jnp.float32)
-    )
+    w_all = jnp.concatenate([w_high, w_low, w_high], axis=0)
+    terms[...] = jnp.dot(map_all[...], w_all, preferred_element_type=jnp.float32)
     to_peer = pltpu.make_async_remote_copy(
         src_ref=terms.at[pl.ds(pl.multiple_of((1 - core) * half, half), half)], dst_ref=halves,
         send_sem=half_sem.at[0], recv_sem=half_sem.at[1],
@@ -257,23 +277,41 @@
     for m in range(MB):
         ker_out[:, m * width : (m + 1) * width] = total[m * TT : (m + 1) * TT]
     everything.wait_send()
+    adj_copy.wait()
+
+
+def hand_over(adj, ker, adj_out, ker_out, sem):
+    first = pltpu.make_async_copy(adj, adj_out, sem.at[0])
+    second = pltpu.make_async_copy(ker, ker_out, sem.at[1])
+    first.start()
+    second.start()
+    first.wait()
+    second.wait()
 
 
 def local(n, records, green, pair_mask, tile_lists, tile_weights, tile_green):
     chips = n // 2
     half = TT * chips
     vmem = pl.BlockSpec(memory_space=pltpu.VMEM)
-    return pl.pallas_call(
+    hbm = pl.BlockSpec(memory_space=pltpu.HBM)
+    adjoint, kernel = pl.pallas_call(
         functools.partial(body, n),
         out_shape=(
             jax.ShapeDtypeStruct((C, 2 * F), jnp.bfloat16),
             jax.ShapeDtypeStruct((TT, CT), jnp.float32),
         ),
-        in_specs=[vmem] * 5 + [pl.BlockSpec(memory_space=pl.ANY)],
-        out_specs=(vmem, vmem),
+        in_specs=[hbm] * 6,
+        out_specs=(hbm, vmem),
         scratch_shapes=[
+            pltpu.VMEM((C, 2 * F), jnp.bfloat16),
+            pltpu.VMEM(records.shape, records.dtype),
+            pltpu.VMEM(green.shape, green.dtype),
+            pltpu.VMEM(pair_mask.shape, pair_mask.dtype),
+            pltpu.VMEM(tile_lists.shape[::-1], tile_lists.dtype),
+            pltpu.VMEM(tile_weights.shape[::-1], tile_weights.dtype),
             pltpu.VMEM((Q, WIN + 1, C, 3 * FC), jnp.bfloat16),
             pltpu.VMEM((C, WIN * C), jnp.bfloat16),
+            pltpu.VMEM((2 * half, 3 * C), jnp.bfloat16),
             pltpu.VMEM((2 * F, CT), jnp.bfloat16),
             pltpu.VMEM((C, CT), jnp.float32),
             pltpu.VMEM((2 * half, CT), jnp.float32),
@@ -283,15 +321,25 @@
             pltpu.VMEM((chips - 1, MB * TT, CT // MB), jnp.bfloat16),
             pltpu.SemaphoreType.DMA((Q, KINDS)),
             pltpu.SemaphoreType.DMA((Q, KINDS)),
-            pltpu.SemaphoreType.DMA,
+            pltpu.SemaphoreType.DMA((7,)),
             pltpu.SemaphoreType.DMA((2,)),
             pltpu.SemaphoreType.DMA((2,)),
         ],
         compiler_params=pltpu.CompilerParams(
-            collective_id=0, has_side_effects=True, vmem_limit_bytes=44 * 2**20
+            collective_id=0, has_side_effects=True, vmem_limit_bytes=56 * 2**20
         ),
         cost_estimate=pl.CostEstimate(flops=10**9, bytes_accessed=6 * 10**6, transcendentals=0),
     )(records, green, pair_mask, tile_lists.T, tile_weights.T, tile_green)
+    return pl.pallas_call(
+        hand_over,
+        out_shape=(
+            jax.ShapeDtypeStruct(adjoint.shape, adjoint.dtype),
+            jax.ShapeDtypeStruct(kernel.shape, kernel.dtype),
+        ),
+        in_specs=[hbm] * 2,
+        out_specs=(hbm, hbm),
+        scratch_shapes=[pltpu.SemaphoreType.DMA((2,))],
+    )(adjoint, kernel)
 
 
 def solution(mesh):

time: 48.6 us -> 53.7 us (1.10)
  Pallas kernels: 39.9 us -> 52.9 us
  local copies, waits for them, and re-layouts: 7.79 us -> 0 us
    pallas_call x0 -> x1, Pallas kernels: none -> 11.5 us  [local(): pl.pallas_call(hand_over, out_shape=(jax.ShapeDtypeStruct(adjoint.shape,...]
    unnamed x14 -> x0, local copies, waits for them, and re-layouts: 7.79 us -> none
    pallas_call x1, Pallas kernels: 39.9 us -> 41.4 us  [local(): pl.pallas_call(functools.partial(body, n), out_shape=(jax.ShapeDtypeStruc...]
where the time goes in v2:
time: 53.7 us; the launch traced here: 53.6 us
  Pallas kernels  52.9 us (99%)
  between operations  0.64 us (1%)
    pallas_call x1, Pallas kernels, local(): pl.pallas_call(functools.partial(body, n), out_shape=(jax.ShapeDtypeStruc...  41.4 us
    pallas_call x1, Pallas kernels, local(): pl.pallas_call(hand_over, out_shape=(jax.ShapeDtypeStruct(adjoint.shape,...  11.5 us

profile of v2, /device:TPU:0, one launch (start us, length us, event | category | flops | bytes accessed | tf_op | source)
XLA Modules:
  0.0 53.6 jit_solution(8870121680839421986)
XLA Ops:
  0.6 41.4 %shard_map.77 = (bf16[80,2048]{1,0:T(8,128)(2,1)}, f32[4,1024]{1,0:T(4,128)}) custom-call(bf16[80,2048]{1,0:T(8,128)(2,1)} %rec_hbm.1, bf16[80,2048]{1,0:T(8,128)(2,1)} %grn_hbm.1, s32[80,720]{1,0:T(8,128)} %mask_hbm.1, s32[16,80]{1,0:T(8,128)} %bitcast.2, f32[16,80]{1,0:T(8,128)} %bitcast.3, bf16[2048,1024]{1,0:T(8,128)(2,1)} %tg_hbm.1), custom_call_target="tpu_custom_call" | custom-call | flops 1000000000 | bytes 6000000 | tf_op jit(solution)/shard_map/pallas_call | solution.py:297
  42.0 11.5 %shard_map.78 = (bf16[80,2048]{1,0:T(8,128)(2,1)}, f32[4,1024]{1,0:T(4,128)}) custom-call(bf16[80,2048]{1,0:T(8,128)(2,1)} %get-tuple-element.4.adj, f32[4,1024]{1,0:T(4,128)} %get-tuple-element.5.ker), custom_call_target="tpu_custom_call" | custom-call | tf_op jit(solution)/shard_map/pallas_call | solution.py:333

commit v3 on v2

--- a/solution.py
+++ b/solution.py
@@ -14,7 +14,8 @@
 CT = 1024
 Q = 8
 FC = F // Q
-AHEAD = 2
+AHEAD = 3
+LAGS = 2, 4, 6
 MB = 4
 MESH = pl.DeviceIdType.MESH
 
@@ -199,17 +200,14 @@
     map_low = (tile_map - map_high.astype(jnp.float32)).astype(jnp.bfloat16)
     map_all[...] = jnp.concatenate([map_high, map_high, map_low], axis=1)
 
-    for step in range(Q + 3):
+    for step in range(Q + LAGS[2]):
         if step < Q:
             stage1(step)
         if step + AHEAD < Q:
             send_own(step + AHEAD)
-        if 0 <= step - 1 < Q:
-            stage2(step - 1)
-        if 0 <= step - 2 < Q:
-            stage3(step - 2)
-        if 0 <= step - 3 < Q:
-            stage4(step - 3)
+        for lag, stage in zip(LAGS, (stage2, stage3, stage4)):
+            if 0 <= step - lag < Q:
+                stage(step - lag)
 
     adj_copy = pltpu.make_async_copy(adj_out, adj_hbm, in_sem.at[6])
     adj_copy.start()
@@ -280,21 +278,12 @@
     adj_copy.wait()
 
 
-def hand_over(adj, ker, adj_out, ker_out, sem):
-    first = pltpu.make_async_copy(adj, adj_out, sem.at[0])
-    second = pltpu.make_async_copy(ker, ker_out, sem.at[1])
-    first.start()
-    second.start()
-    first.wait()
-    second.wait()
-
-
 def local(n, records, green, pair_mask, tile_lists, tile_weights, tile_green):
     chips = n // 2
     half = TT * chips
     vmem = pl.BlockSpec(memory_space=pltpu.VMEM)
     hbm = pl.BlockSpec(memory_space=pltpu.HBM)
-    adjoint, kernel = pl.pallas_call(
+    return pl.pallas_call(
         functools.partial(body, n),
         out_shape=(
             jax.ShapeDtypeStruct((C, 2 * F), jnp.bfloat16),
@@ -330,16 +319,6 @@
         ),
         cost_estimate=pl.CostEstimate(flops=10**9, bytes_accessed=6 * 10**6, transcendentals=0),
     )(records, green, pair_mask, tile_lists.T, tile_weights.T, tile_green)
-    return pl.pallas_call(
-        hand_over,
-        out_shape=(
-            jax.ShapeDtypeStruct(adjoint.shape, adjoint.dtype),
-            jax.ShapeDtypeStruct(kernel.shape, kernel.dtype),
-        ),
-        in_specs=[hbm] * 2,
-        out_specs=(hbm, hbm),
-        scratch_shapes=[pltpu.SemaphoreType.DMA((2,))],
-    )(adjoint, kernel)
 
 
 def solution(mesh):

time: 53.7 us -> 42.2 us (0.79)
  Pallas kernels: 52.9 us -> 38.2 us
  local copies, waits for them, and re-layouts: 0 us -> 3.04 us
    pallas_call x1 -> x0, Pallas kernels: 11.5 us -> none  [local(): pl.pallas_call(hand_over, out_shape=(jax.ShapeDtypeStruct(adjoint.shape,...]
    pallas_call x1, Pallas kernels: 41.4 us -> 38.2 us  [local(): pl.pallas_call(functools.partial(body, n), out_shape=(jax.ShapeDtypeStruc...]
    unnamed x0 -> x2, local copies, waits for them, and re-layouts: none -> 3.04 us
where the time goes in v3:
time: 42.2 us; the launch traced here: 41.9 us
  Pallas kernels  38.2 us (91%)
  local copies, waits for them, and re-layouts  3.04 us (7%)
  between operations  0.64 us (2%)
    pallas_call x1, Pallas kernels, local(): pl.pallas_call(functools.partial(body, n), out_shape=(jax.ShapeDtypeStruc...  38.2 us
    unnamed x2, local copies, waits for them, and re-layouts  3.04 us

profile of v3, /device:TPU:0, one launch (start us, length us, event | category | flops | bytes accessed | tf_op | source)
XLA Modules:
  0.0 41.9 jit_solution(4645678866433188837)
XLA Ops:
  0.6 38.2 %shard_map.77 = (bf16[80,2048]{1,0:T(8,128)(2,1)}, f32[4,1024]{1,0:T(4,128)}) custom-call(bf16[80,2048]{1,0:T(8,128)(2,1)} %rec_hbm.1, bf16[80,2048]{1,0:T(8,128)(2,1)} %grn_hbm.1, s32[80,720]{1,0:T(8,128)} %mask_hbm.1, s32[16,80]{1,0:T(8,128)} %bitcast.2, f32[16,80]{1,0:T(8,128)} %bitcast.3, bf16[2048,1024]{1,0:T(8,128)(2,1)} %tg_hbm.1), custom_call_target="tpu_custom_call" | custom-call | flops 1000000000 | bytes 6000000 | tf_op jit(solution)/shard_map/pallas_call | solution.py:286
  38.9 1.7 %copy.10 = bf16[80,2048]{1,0:T(8,128)(2,1)} copy(bf16[80,2048]{1,0:T(8,128)(2,1)} %get-tuple-element.4) | data formatting | bytes 655360
  40.6 1.3 %copy.11 = f32[4,1024]{1,0:T(4,128)} copy(f32[4,1024]{1,0:T(4,128)} %get-tuple-element.5) | data formatting | bytes 32768

commit v4 on v3

--- a/solution.py
+++ b/solution.py
@@ -15,7 +15,7 @@
 Q = 8
 FC = F // Q
 AHEAD = 3
-LAGS = 2, 4, 6
+LAGS = 2, 4, 5
 MB = 4
 MESH = pl.DeviceIdType.MESH
 
@@ -25,8 +25,8 @@
 
 
 def body(
-    n, rec_hbm, grn_hbm, mask_hbm, lists_hbm, weights_hbm, tg_hbm, adj_hbm, ker_out,
-    adj_out, rec, grn, mask, lists, weights, buf, mask_bf, map_all, tg, w_acc, terms, halves, wide, packed, landed,
+    n, rec_hbm, grn_hbm, mask_hbm, lists_hbm, weights_hbm, tg_hbm, adj_out, ker_out,
+    rec, grn, mask, lists, weights, buf, mask_bf, map_all, tg, w_acc, terms, halves, wide, packed, landed,
     send_sem, recv_sem, in_sem, half_sem, sum_sem,
 ):
     chips = n // 2
@@ -169,10 +169,11 @@
         adj_out[:, F + q * FC : F + (q + 1) * FC] = imag
         if q == 0:
             fetches[5].wait()
+        rows = jnp.concatenate(
+            [tg[q * FC : (q + 1) * FC, :], tg[F + q * FC : F + (q + 1) * FC, :]], axis=0
+        )
         more = jnp.dot(
-            real, tg[q * FC : (q + 1) * FC, :], preferred_element_type=jnp.float32
-        ) + jnp.dot(
-            imag, tg[F + q * FC : F + (q + 1) * FC, :], preferred_element_type=jnp.float32
+            jnp.concatenate([real, imag], axis=1), rows, preferred_element_type=jnp.float32
         )
         w_acc[...] = more if q == 0 else w_acc[...] + more
 
@@ -209,9 +210,6 @@
             if 0 <= step - lag < Q:
                 stage(step - lag)
 
-    adj_copy = pltpu.make_async_copy(adj_out, adj_hbm, in_sem.at[6])
-    adj_copy.start()
-
     w = w_acc[...]
     w_high = w.astype(jnp.bfloat16)
     w_low = (w - w_high.astype(jnp.float32)).astype(jnp.bfloat16)
@@ -275,7 +273,6 @@
     for m in range(MB):
         ker_out[:, m * width : (m + 1) * width] = total[m * TT : (m + 1) * TT]
     everything.wait_send()
-    adj_copy.wait()
 
 
 def local(n, records, green, pair_mask, tile_lists, tile_weights, tile_green):
@@ -290,9 +287,8 @@
             jax.ShapeDtypeStruct((TT, CT), jnp.float32),
         ),
         in_specs=[hbm] * 6,
-        out_specs=(hbm, vmem),
+        out_specs=(vmem, vmem),
         scratch_shapes=[
-            pltpu.VMEM((C, 2 * F), jnp.bfloat16),
             pltpu.VMEM(records.shape, records.dtype),
             pltpu.VMEM(green.shape, green.dtype),
             pltpu.VMEM(pair_mask.shape, pair_mask.dtype),
@@ -310,12 +306,12 @@
             pltpu.VMEM((chips - 1, MB * TT, CT // MB), jnp.bfloat16),
             pltpu.SemaphoreType.DMA((Q, KINDS)),
             pltpu.SemaphoreType.DMA((Q, KINDS)),
-            pltpu.SemaphoreType.DMA((7,)),
+            pltpu.SemaphoreType.DMA((6,)),
             pltpu.SemaphoreType.DMA((2,)),
             pltpu.SemaphoreType.DMA((2,)),
         ],
         compiler_params=pltpu.CompilerParams(
-            collective_id=0, has_side_effects=True, vmem_limit_bytes=56 * 2**20
+            collective_id=0, has_side_effects=True, vmem_limit_bytes=40 * 2**20
         ),
         cost_estimate=pl.CostEstimate(flops=10**9, bytes_accessed=6 * 10**6, transcendentals=0),
     )(records, green, pair_mask, tile_lists.T, tile_weights.T, tile_green)

time: 42.2 us -> 46.3 us (1.097)
  local copies, waits for them, and re-layouts: 3.04 us -> 7.79 us
  Pallas kernels: 38.2 us -> 37.5 us
    unnamed x2 -> x14, local copies, waits for them, and re-layouts: 3.04 us -> 7.79 us
    pallas_call x1, Pallas kernels: 38.2 us -> 37.5 us  [local(): pl.pallas_call(functools.partial(body, n), out_shape=(jax.ShapeDtypeStruc...]
where the time goes in v4:
time: 46.3 us; the launch traced here: 45.9 us
  Pallas kernels  37.5 us (81%)
  local copies, waits for them, and re-layouts  7.79 us (17%)
  between operations  0.65 us (1%)
    pallas_call x1, Pallas kernels, local(): pl.pallas_call(functools.partial(body, n), out_shape=(jax.ShapeDtypeStruc...  37.5 us
    unnamed x14, local copies, waits for them, and re-layouts  7.79 us

profile of v4, /device:TPU:0, one launch (start us, length us, event | category | flops | bytes accessed | tf_op | source)
XLA Modules:
  0.0 45.9 jit_solution(15177766842153311917)
XLA Ops:
  0.6 0.0 copy-start
  0.6 2.2 %copy-done = bf16[2048,1024]{1,0:T(8,128)(2,1)S(1)} copy-done((bf16[2048,1024]{1,0:T(8,128)(2,1)S(1)}, bf16[2048,1024]{1,0:T(8,128)(2,1)}, u32[]{:S(2)}) %copy-start) | copy-done | bytes 4194328
  2.8 0.0 copy-start.1
  2.8 1.0 %copy-done.1 = bf16[80,2048]{1,0:T(8,128)(2,1)S(1)} copy-done((bf16[80,2048]{1,0:T(8,128)(2,1)S(1)}, bf16[80,2048]{1,0:T(8,128)(2,1)}, u32[]{:S(2)}) %copy-start.1) | copy-done | bytes 327704
  3.8 0.0 copy-start.2
  3.8 1.0 %copy-done.2 = bf16[80,2048]{1,0:T(8,128)(2,1)S(1)} copy-done((bf16[80,2048]{1,0:T(8,128)(2,1)S(1)}, bf16[80,2048]{1,0:T(8,128)(2,1)}, u32[]{:S(2)}) %copy-start.2) | copy-done | bytes 327704
  4.8 0.0 copy-start.3
  4.8 0.9 %copy-done.3 = s32[80,720]{1,0:T(8,128)S(1)} copy-done((s32[80,720]{1,0:T(8,128)S(1)}, s32[80,720]{1,0:T(8,128)}, u32[]{:S(2)}) %copy-start.3) | copy-done | bytes 230424
  5.7 0.0 copy-start.4
  5.7 0.7 %copy-done.4 = s32[80,16]{0,1:T(8,128)S(1)} copy-done((s32[80,16]{0,1:T(8,128)S(1)}, s32[80,16]{0,1:T(8,128)}, u32[]{:S(2)}) %copy-start.4) | copy-done | bytes 5144
  6.4 0.0 copy-start.5
  6.4 0.7 %copy-done.5 = f32[80,16]{0,1:T(8,128)S(1)} copy-done((f32[80,16]{0,1:T(8,128)S(1)}, f32[80,16]{0,1:T(8,128)}, u32[]{:S(2)}) %copy-start.5) | copy-done | bytes 5144
  7.1 37.5 %shard_map.77 = (bf16[80,2048]{1,0:T(8,128)(2,1)S(1)}, f32[4,1024]{1,0:T(4,128)S(1)}) custom-call(bf16[80,2048]{1,0:T(8,128)(2,1)S(1)} %copy-done.1, bf16[80,2048]{1,0:T(8,128)(2,1)S(1)} %copy-done.2, s32[80,720]{1,0:T(8,128)S(1)} %copy-done.3, s32[16,80]{1,0:T(8,128)S(1)} %bitcast.2, f32[16,80]{1,0:T(8,128)S(1)} %bitcast.3, bf16[2048,1024]{1,0:T(8,128)(2,1)S(1)} %copy-done), custom_call_target="tpu_custom_call" | custom-call | flops 1000000000 | bytes 6000000 | tf_op jit(solution)/shard_map/pallas_call | solution.py:283
  44.6 0.7 %copy.10 = bf16[80,2048]{1,0:T(8,128)(2,1)} copy(bf16[80,2048]{1,0:T(8,128)(2,1)S(1)} %get-tuple-element.4) | data formatting | bytes 655360
  45.3 0.6 %copy.11 = f32[4,1024]{1,0:T(4,128)} copy(f32[4,1024]{1,0:T(4,128)S(1)} %get-tuple-element.5) | data formatting | bytes 32768
Async XLA Ops:
  0.6 2.2 %copy-start = (bf16[2048,1024]{1,0:T(8,128)(2,1)S(1)}, bf16[2048,1024]{1,0:T(8,128)(2,1)}, u32[]{:S(2)}) copy-start(bf16[2048,1024]{1,0:T(8,128)(2,1)} %tg_hbm.1) | copy-start | bytes 12582916
  2.8 1.0 %copy-start.1 = (bf16[80,2048]{1,0:T(8,128)(2,1)S(1)}, bf16[80,2048]{1,0:T(8,128)(2,1)}, u32[]{:S(2)}) copy-start(bf16[80,2048]{1,0:T(8,128)(2,1)} %rec_hbm.1) | copy-start | bytes 983044
  3.8 1.0 %copy-start.2 = (bf16[80,2048]{1,0:T(8,128)(2,1)S(1)}, bf16[80,2048]{1,0:T(8,128)(2,1)}, u32[]{:S(2)}) copy-start(bf16[80,2048]{1,0:T(8,128)(2,1)} %grn_hbm.1) | copy-start | bytes 983044
  4.8 0.9 %copy-start.3 = (s32[80,720]{1,0:T(8,128)S(1)}, s32[80,720]{1,0:T(8,128)}, u32[]{:S(2)}) copy-start(s32[80,720]{1,0:T(8,128)} %mask_hbm.1) | copy-start | bytes 691204
  5.7 0.7 %copy-start.4 = (s32[80,16]{0,1:T(8,128)S(1)}, s32[80,16]{0,1:T(8,128)}, u32[]{:S(2)}) copy-start(s32[80,16]{0,1:T(8,128)} %param.9) | copy-start | bytes 15364
  6.4 0.7 %copy-start.5 = (f32[80,16]{0,1:T(8,128)S(1)}, f32[80,16]{0,1:T(8,128)}, u32[]{:S(2)}) copy-start(f32[80,16]{0,1:T(8,128)} %param.10) | copy-start | bytes 15364

commit v5 on v4

--- a/solution.py
+++ b/solution.py
@@ -14,8 +14,8 @@
 CT = 1024
 Q = 8
 FC = F // Q
-AHEAD = 3
-LAGS = 2, 4, 5
+AHEAD = 4
+LAGS = 3, 5, 6
 MB = 4
 MESH = pl.DeviceIdType.MESH
 
@@ -283,8 +283,8 @@
     return pl.pallas_call(
         functools.partial(body, n),
         out_shape=(
-            jax.ShapeDtypeStruct((C, 2 * F), jnp.bfloat16),
-            jax.ShapeDtypeStruct((TT, CT), jnp.float32),
+            pltpu.VMEM((C, 2 * F), jnp.bfloat16),
+            pltpu.VMEM((TT, CT), jnp.float32),
         ),
         in_specs=[hbm] * 6,
         out_specs=(vmem, vmem),
@@ -314,7 +314,12 @@
             collective_id=0, has_side_effects=True, vmem_limit_bytes=40 * 2**20
         ),
         cost_estimate=pl.CostEstimate(flops=10**9, bytes_accessed=6 * 10**6, transcendentals=0),
-    )(records, green, pair_mask, tile_lists.T, tile_weights.T, tile_green)
+    )(
+        *(
+            pltpu.with_memory_space_constraint(value, pltpu.HBM)
+            for value in (records, green, pair_mask, tile_lists.T, tile_weights.T, tile_green)
+        )
+    )
 
 
 def solution(mesh):

time: 46.3 us -> 39.8 us (0.86)
  local copies, waits for them, and re-layouts: 7.79 us -> 1.33 us
    unnamed x14 -> x2, local copies, waits for them, and re-layouts: 7.79 us -> 1.33 us
where the time goes in v5:
time: 39.8 us; the launch traced here: 39.1 us
  Pallas kernels  37.2 us (93%)
  local copies, waits for them, and re-layouts  1.33 us (3%)
  between operations  0.64 us (2%)
    pallas_call x1, Pallas kernels, local(): pl.pallas_call(functools.partial(body, n), out_shape=(pltpu.VMEM((C, 2 *...  37.2 us
    unnamed x2, local copies, waits for them, and re-layouts  1.33 us

profile of v5, /device:TPU:0, one launch (start us, length us, event | category | flops | bytes accessed | tf_op | source)
XLA Modules:
  0.0 39.1 jit_solution(12650737790528059022)
XLA Ops:
  0.6 37.2 %shard_map.77 = (bf16[80,2048]{1,0:T(8,128)(2,1)S(1)}, f32[4,1024]{1,0:T(4,128)S(1)}) custom-call(bf16[80,2048]{1,0:T(8,128)(2,1)} %rec_hbm.1, bf16[80,2048]{1,0:T(8,128)(2,1)} %grn_hbm.1, s32[80,720]{1,0:T(8,128)} %mask_hbm.1, s32[16,80]{1,0:T(8,128)} %bitcast.2, f32[16,80]{1,0:T(8,128)} %bitcast.3, bf16[2048,1024]{1,0:T(8,128)(2,1)} %tg_hbm.1), custom_call_target="tpu_custom_call" | custom-call | flops 1000000000 | bytes 6000000 | tf_op jit(solution)/shard_map/pallas_call | solution.py:283
  37.8 0.7 %copy.10 = bf16[80,2048]{1,0:T(8,128)(2,1)} copy(bf16[80,2048]{1,0:T(8,128)(2,1)S(1)} %get-tuple-element.2) | data formatting | bytes 655360
  38.5 0.6 %copy.11 = f32[4,1024]{1,0:T(4,128)} copy(f32[4,1024]{1,0:T(4,128)S(1)} %get-tuple-element.3) | data formatting | bytes 32768

commit v6 on v5

--- a/solution.py
+++ b/solution.py
@@ -14,8 +14,8 @@
 CT = 1024
 Q = 8
 FC = F // Q
-AHEAD = 4
-LAGS = 3, 5, 6
+AHEAD = 3
+LAGS = 2, 4, 5
 MB = 4
 MESH = pl.DeviceIdType.MESH
 
@@ -100,31 +100,45 @@
         move(q, 4, 4, kind, kind, peer).wait_send()
 
     def send_own(q):
+        @pl.when(is1)
+        def _():
+            move(q, 4, slot_v, X, X, x_dev).start()
+
         move(q, 4, slot_z, Y, Y, y_dev).start()
-        move(q, 4, slot_v, X, X, x_dev).start()
+
+        @pl.when(is0)
+        def _():
+            move(q, 4, slot_v, X, X, x_dev).start()
+
         relay(q, 4, 0).start()
 
     def stage1(q):
+        @pl.when(is1)
+        def _():
+            arrived(q, slot_x, X)
+
+            @pl.when(inner == 0)
+            def _():
+                move(q, slot_x, slot_v, V, V, y_dev).start()
+
+            @pl.when(inner == 1)
+            def _():
+                move(q, slot_x, TRANSIT, V, T, y_dev).start()
+
         arrived(q, slot_y, Y)
         move(q, slot_y, slot_z, Z, Z, z_dev).start()
 
+        @pl.when(is0 & (inner == 0))
+        def _():
+            move(q, slot_y, slot_x, V, V, x_dev).start()
+
         @pl.when(core == upper)
         def _():
             relay(q, slot_y, 3).start()
 
-        @pl.when(is0 & (inner == 0))
-        def _():
-            move(q, slot_y, slot_x, V, V, x_dev).start()
-
-        arrived(q, slot_x, X)
-
-        @pl.when(is1 & (inner == 0))
-        def _():
-            move(q, slot_x, slot_v, V, V, y_dev).start()
-
-        @pl.when(is1 & (inner == 1))
-        def _():
-            move(q, slot_x, TRANSIT, V, T, y_dev).start()
+        @pl.when(is0)
+        def _():
+            arrived(q, slot_x, X)
 
         relay(q, slot_x, 1).start()
 

time: 39.8 us -> 39.4 us (0.990); the launches traced: 39.1 us -> 39.3 us
  no operation moved by 1% of the time
where the time goes in v6:
time: 39.4 us; the launch traced here: 39.3 us
  Pallas kernels  37.3 us (95%)
  local copies, waits for them, and re-layouts  1.33 us (3%)
  between operations  0.64 us (2%)
    pallas_call x1, Pallas kernels, local(): pl.pallas_call(functools.partial(body, n), out_shape=(pltpu.VMEM((C, 2 *...  37.3 us
    unnamed x2, local copies, waits for them, and re-layouts  1.33 us

profile of v6, /device:TPU:0, one launch (start us, length us, event | category | flops | bytes accessed | tf_op | source)
XLA Modules:
  0.0 39.3 jit_solution(12115491345665434426)
XLA Ops:
  0.6 37.3 %shard_map.77 = (bf16[80,2048]{1,0:T(8,128)(2,1)S(1)}, f32[4,1024]{1,0:T(4,128)S(1)}) custom-call(bf16[80,2048]{1,0:T(8,128)(2,1)} %rec_hbm.1, bf16[80,2048]{1,0:T(8,128)(2,1)} %grn_hbm.1, s32[80,720]{1,0:T(8,128)} %mask_hbm.1, s32[16,80]{1,0:T(8,128)} %bitcast.2, f32[16,80]{1,0:T(8,128)} %bitcast.3, bf16[2048,1024]{1,0:T(8,128)(2,1)} %tg_hbm.1), custom_call_target="tpu_custom_call" | custom-call | flops 1000000000 | bytes 6000000 | tf_op jit(solution)/shard_map/pallas_call | solution.py:297
  37.9 0.7 %copy.10 = bf16[80,2048]{1,0:T(8,128)(2,1)} copy(bf16[80,2048]{1,0:T(8,128)(2,1)S(1)} %get-tuple-element.2) | data formatting | bytes 655360
  38.7 0.6 %copy.11 = f32[4,1024]{1,0:T(4,128)} copy(f32[4,1024]{1,0:T(4,128)S(1)} %get-tuple-element.3) | data formatting | bytes 32768
